TPU v7x, 32 devices: a whole 2x2x4 slice. The times are simulated.
32 devices in a mesh: row: 4 (over x, core), col: 2 (over y), layer: 4 (over z).
Axes of the slice: x: 2, y: 2, z: 4, core: 2. Of those that a mesh axis runs over, the one named last changes fastest.
Arguments:
- a_vals: bfloat16 [4, 2, 4, 32, 4096], P('row', 'col', 'layer'), may hold values from -6 to 6
- a_rows: int32 [4, 2, 4, 32], P('row', 'col', 'layer'), may hold values from 0 to 7, as said below
- a_cols: int32 [4, 2, 4, 32], P('row', 'col', 'layer'), may hold values from 0 to 15, as said below
- a_count: int32 [4, 2, 4], P('row', 'col', 'layer'), may hold values from 8 to 32, as said below
- p_vals: bfloat16 [4, 2, 4, 32, 4096], P('row', 'col', 'layer'), may hold values from -0.1875 to 0.1875
- p_rows: int32 [4, 2, 4, 32], P('row', 'col', 'layer'), may hold values from 0 to 7, as said below
- p_cols: int32 [4, 2, 4, 32], P('row', 'col', 'layer'), may hold values from 0 to 7, as said below
- p_count: int32 [4, 2, 4], P('row', 'col', 'layer'), may hold values from 16 to 32, as said below
Outputs:
- galerkin: float32 [2048, 1024], P('row', ('col', 'layer'))
Inputs may be any that keep to these rules, and one draw needn't show every extreme that they name: Within one tile the slots name distinct blocks; a_rows indexes the 8 block rows of the tile. a_cols indexes the 16 inner block columns of the tile. Slots from a_count on are unused; some tile uses all 32 slots and some the fewest. Within one tile the slots name distinct blocks; p_rows indexes the 8 inner block rows of the tile. p_cols indexes the 8 coarse block columns of the tile. Slots from p_count on are unused; some tile uses all 32 slots and some the fewest.
All inputs are finite; a program needn't handle non-finite values.
Results may differ from a plain program's by a relative error of at most 0.0003.
Values may be sent and summed in bfloat16 or wider, within the bound.
A program may use at most 128 MiB of HBM per device.

v0:
```python
import functools

import jax
import jax.numpy as jnp
from jax import lax
from jax.experimental import pallas as pl
from jax.experimental.pallas import tpu as pltpu
from jax.sharding import PartitionSpec as P

BS = 64
RB = 8
KB = 16
JB = 8
LANES = 128
MESH = pl.DeviceIdType.MESH
F32 = jnp.float32
BF16 = jnp.bfloat16


def positions(rows, cols, count, width):
    slot = lax.broadcasted_iota(jnp.int32, rows.shape, 1)
    pos = jnp.where(slot < count, rows * width + cols, -1)
    row = jnp.concatenate([pos] * (LANES // pos.shape[1]), axis=1)
    return jnp.broadcast_to(row, (8, LANES))


def pair_onehot(pos, pairs, width, slots):
    shape = (pairs * 8, 2 * slots)
    row = lax.broadcasted_iota(jnp.int32, shape, 0)
    lane = lax.broadcasted_iota(jnp.int32, shape, 1)
    want = (row % 8) * width + 2 * (row // 8) + lane // slots
    return jnp.where(want == pos[0:1, : 2 * slots], 1.0, 0.0).astype(BF16)


def spread(vals, onehot, pairs, store, first=0, last=8):
    slots = vals.shape[0]
    low = lax.broadcasted_iota(jnp.int32, (slots, LANES), 1) < BS

    def body(step, carry):
        v = vals[:, pl.ds(pl.multiple_of(step * 512, 512), 512)].astype(F32)
        parts = []
        for g in range(4):
            a = v[:, g * LANES : (g + 1) * LANES]
            b = pltpu.roll(a, BS, 1)
            parts.append(jnp.concatenate([jnp.where(low, a, 0.0), jnp.where(low, 0.0, b)], axis=0))
            parts.append(jnp.concatenate([jnp.where(low, b, 0.0), jnp.where(low, 0.0, a)], axis=0))
        w = jnp.concatenate(parts, axis=1).astype(BF16)
        d = jnp.dot(onehot, w, preferred_element_type=F32)
        for p in range(pairs):
            rows = [d[p * 8 : (p + 1) * 8, i * LANES : (i + 1) * LANES] for i in range(8)]
            store(step, p, jnp.concatenate(rows, axis=0).astype(BF16))
        return carry

    lax.fori_loop(first, last, body, 0, unroll=True)


def kernel(
    n_row, n_col, n_layer, a_hbm, p_hbm, *rest,
):
    small_hbm, out, small, scratch = rest[:6], rest[6], rest[7:13], rest[13:]
    (
    a_buf, p_buf, a_pos, p_pos, a_own_pos, p_own_pos, a_dense, a_mixed, p_dense, order, acc, code, code_in, peak, peak_in,
    loc_sem, a_send, a_recv, ap_send, ap_recv, p_send, p_recv, r_send, r_recv, s_send, s_recv, pp_send, pp_recv,
    c_send, c_recv, m_send, m_recv,
    ) = scratch
    row, col, lay = lax.axis_index("row"), lax.axis_index("col"), lax.axis_index("layer")
    core = lax.rem(row, 2)
    sib = row + 1 - 2 * core
    chips = n_row // 2
    half = BS * BS // 2
    slots = a_hbm.shape[0]

    own_a = pltpu.make_async_copy(a_hbm, a_buf.at[0], loc_sem.at[0])
    own_p = pltpu.make_async_copy(p_hbm, p_buf.at[0], loc_sem.at[1])
    tables = [pltpu.make_async_copy(small_hbm[k], small[k], loc_sem.at[2 + k]) for k in range(6)]
    for copy in tables:
        copy.start()
    own_p.start()
    own_a.start()
    barrier = pltpu.get_barrier_semaphore()
    for d in range(1, n_row):
        pl.semaphore_signal(barrier, inc=1, device_id={"row": lax.rem(row + d, n_row)}, device_id_type=MESH)
    for d in range(1, n_col):
        pl.semaphore_signal(barrier, inc=1, device_id={"col": lax.rem(col + d, n_col)}, device_id_type=MESH)
    for d in range(1, n_layer):
        pl.semaphore_signal(barrier, inc=1, device_id={"layer": lax.rem(lay + d, n_layer)}, device_id_type=MESH)
    pl.semaphore_wait(barrier, n_row + n_col + n_layer - 3)

    def remote(src, dst, send, recv, where):
        return pltpu.make_async_remote_copy(
            src_ref=src, dst_ref=dst, send_sem=send, recv_sem=recv, device_id=where, device_id_type=MESH
        )

    def piece(ref, h):
        return ref.at[:, pl.ds(h * half, half)]

    across, relay = {}, {}
    for h in range(2):
        for d in range(1, chips):
            to = lax.rem(row + 2 * d, n_row)
            across[d, h] = remote(
                piece(p_hbm, h), piece(p_buf.at[2 * d], h), p_send.at[d, h], p_recv.at[d, h], {"row": to}
            )
            relay[d, h] = remote(
                piece(p_buf.at[2 * d], h), piece(p_buf.at[2 * d + 1], h), r_send.at[d, h], r_recv.at[d, h], {"row": sib}
            )
            if h == 0:
                across[d, h].start()
    over = {}
    for d in range(1, n_col):
        to = {"col": lax.rem(col + d, n_col)}
        for h in range(2):
            over[d, h] = remote(piece(a_hbm, h), piece(a_buf.at[d], h), a_send.at[d, h], a_recv.at[d, h], to)
            if h == 0:
                over[d, h].start()
    for copy in tables:
        copy.wait()
    a_rows, a_cols, a_count, p_rows, p_cols, p_count = small
    a_own_pos[...] = positions(a_rows[...], a_cols[...], a_count[...], KB)
    p_own_pos[...] = positions(p_rows[...], p_cols[...], p_count[...], JB)
    over_marks = {}
    for d in range(1, n_col):
        to = {"col": lax.rem(col + d, n_col)}
        over_marks[d] = remote(a_own_pos, a_pos.at[d], ap_send.at[d], ap_recv.at[d], to)
        over_marks[d].start()
    marks = []
    for d in range(1, n_row):
        if d % 2 == 0:
            to = lax.rem(row + d, n_row)
        else:
            to = lax.rem(sib + d - 1, n_row)
        marks.append(remote(p_own_pos, p_pos.at[d], pp_send.at[d], pp_recv.at[d], {"row": to}))
        marks[-1].start()
    beside = remote(p_hbm, p_buf.at[1], s_send, s_recv, {"row": sib})
    beside.start()
    for d in range(1, chips):
        across[d, 1].start()
    for d in range(1, n_col):
        over[d, 1].start()

    shape = order.shape
    r = lax.broadcasted_iota(jnp.int32, shape, 0)
    c = lax.broadcasted_iota(jnp.int32, shape, 1)
    order[...] = jnp.where(c == (r % BS) * 8 + r // BS, 1.0, 0.0).astype(BF16)

    def take_a(d, h):
        pos = a_own_pos if d == 0 else a_pos.at[d]
        onehot = pair_onehot(pos[...], KB // 2, KB, slots)
        first = 2 * lax.rem(col - d + n_col, n_col)

        def store(step, p, rows):
            lanes = pl.ds((p % 4) * LANES, LANES)
            a_mixed[p // 4, pl.ds(pl.multiple_of(step * 64, 64), 64), lanes] = rows

        spread(a_buf.at[d], onehot, KB // 2, store, 4 * h, 4 * h + 4)
        rows = pl.ds(h * 256, 256)
        for q in range(2):
            a_dense[first + q, rows, :] = jnp.dot(
                a_mixed[q, rows, :], order[...], preferred_element_type=F32
            ).astype(BF16)

    def take_p(d, h):
        pos = p_own_pos if d == 0 else p_pos.at[d]
        onehot = pair_onehot(pos[...], JB // 2, JB, slots)

        def store(step, p, rows):
            p_dense[d, pl.ds(pl.multiple_of(step * 64, 64), 64), p * LANES : (p + 1) * LANES] = rows

        spread(p_buf.at[d], onehot, JB // 2, store, 4 * h, 4 * h + 4)

    def source(d):
        base = row if d % 2 == 0 else sib
        return lax.rem(base - 2 * (d // 2) + n_row, n_row)

    own_p.wait()
    take_p(0, 0)
    take_p(0, 1)
    own_a.wait()
    take_a(0, 0)
    take_a(0, 1)
    beside.wait_recv()
    marks[0].wait_recv()
    take_p(1, 0)
    take_p(1, 1)
    for h in range(2):
        for d in range(1, chips):
            across[d, h].wait_recv()
            relay[d, h].start()
        for d in range(1, n_col):
            if h == 0:
                over_marks[d].wait_recv()
            over[d, h].wait_recv()
            take_a(d, h)
        rows = pl.ds(h * 256, 256)
        acc[rows, :] = jnp.dot(a_dense[source(0), rows, :], p_dense[0], preferred_element_type=F32) + jnp.dot(
            a_dense[source(1), rows, :], p_dense[1], preferred_element_type=F32
        )
        if h == 0:
            for d in range(2, n_row):
                marks[d - 1].wait_recv()
                if d % 2:
                    relay[d // 2, 0].wait_recv()
                take_p(d, 0)
    for d in range(2, n_row):
        if d % 2:
            relay[d // 2, 1].wait_recv()
        take_p(d, 1)
        acc[...] += jnp.dot(a_dense[source(d)], p_dense[d], preferred_element_type=F32)

    def mine(to):
        return acc[:, pl.ds(pl.multiple_of(to * LANES, LANES), LANES)].reshape(BS, 8, LANES)

    def encode(k, x):
        top = jnp.maximum(jnp.max(jnp.abs(x), axis=0), 1.2e-38)
        peak[k] = top
        q = jnp.round((x * (1.0 / top)) * 32767.0)
        code[k] = q.astype(jnp.int32).astype(jnp.int16).reshape(BS * 8, LANES)

    def decode(k):
        q = code_in[k].astype(jnp.int32).astype(F32).reshape(BS, 8, LANES)
        return (q * (1.0 / 32767.0)) * peak_in[k]

    def hand(k, slot, to):
        where = {"layer": to}
        return (
            remote(code.at[k], code_in.at[slot], c_send.at[k], c_recv.at[slot], where),
            remote(peak.at[k], peak_in.at[slot], m_send.at[k], m_recv.at[slot], where),
        )

    def start(copies):
        for copy in copies:
            copy.start()

    def arrive(copies):
        for copy in copies:
            copy.wait_recv()

    sums = []
    if n_layer == 4:
        inner = jnp.logical_or(lay == 1, lay == 2)
        near = lay + 1 - 2 * lax.rem(lay, 2)
        far = lax.rem(lay + 2, 4)
        across_to = 3 - lay
        via = hand(0, jnp.where(inner, 3, 0), jnp.where(inner, across_to, near))
        by_far, by_near = hand(2, 2, far), hand(1, 1, near)
        taken = hand(0, 0, near)
        third = hand(0, 3, across_to)
        sums = list(via) + list(by_far) + list(by_near)

        encode(0, mine(across_to))
        start(via)

        @pl.when(jnp.logical_not(inner))
        def _():
            encode(2, mine(far))
            start(by_far)

        encode(1, mine(near))
        start(by_near)

        @pl.when(inner)
        def _():
            arrive(taken)
            encode(2, mine(far) + decode(0))
            start(by_far)
            arrive(third)
            out[...] = mine(lay) + decode(3)

        @pl.when(jnp.logical_not(inner))
        def _():
            out[...] = mine(lay)

        arrive(by_near)
        total = out[...] + decode(1)
        arrive(by_far)
        total = total + decode(2)
    else:
        for d in range(n_layer - 1, 0, -1):
            to = lax.rem(lay + d, n_layer)
            encode(d, mine(to))
            copies = hand(d, d, to)
            start(copies)
            sums.extend(copies)
        total = mine(lay)
        for d in range(n_layer - 1, 0, -1):
            arrive(hand(d, d, lax.rem(lay + d, n_layer)))
            total = total + decode(d)
    out[...] = total

    for h in range(2):
        for d in range(1, chips):
            across[d, h].wait_send()
            relay[d, h].wait_send()
    for copy in list(over.values()) + list(over_marks.values()) + marks + sums + [beside]:
        copy.wait_send()


def solution(mesh):
    n_row, n_col, n_layer = (mesh.shape[k] for k in ("row", "col", "layer"))

    def on_device(a_vals, a_rows, a_cols, a_count, p_vals, p_rows, p_cols, p_count):
        slots = a_vals.shape[3]
        wide = BS * BS
        any_space = pl.BlockSpec(memory_space=pltpu.HBM)
        vmem = pl.BlockSpec(memory_space=pltpu.VMEM)
        dma = pltpu.SemaphoreType.DMA
        chips = n_row // 2
        got = pl.pallas_call(
            functools.partial(kernel, n_row, n_col, n_layer),
            out_shape=jax.ShapeDtypeStruct((BS, RB, LANES), F32),
            in_specs=[any_space] * 8,
            out_specs=vmem,
            scratch_shapes=(
                [pltpu.VMEM((1, slots), jnp.int32)] * 2 + [pltpu.VMEM((1, 1), jnp.int32)]
            ) * 2 + [
                pltpu.VMEM((n_col, slots, wide), BF16),
                pltpu.VMEM((n_row, slots, wide), BF16),
                pltpu.VMEM((n_col, 8, LANES), jnp.int32),
                pltpu.VMEM((n_row, 8, LANES), jnp.int32),
                pltpu.VMEM((8, LANES), jnp.int32),
                pltpu.VMEM((8, LANES), jnp.int32),
                pltpu.VMEM((n_row, RB * BS, 8 * BS), BF16),
                pltpu.VMEM((2, RB * BS, 8 * BS), BF16),
                pltpu.VMEM((n_row, 8 * BS, JB * BS), BF16),
                pltpu.VMEM((8 * BS, 8 * BS), BF16),
                pltpu.VMEM((RB * BS, JB * BS), F32),
                pltpu.VMEM((n_layer, RB * BS, LANES), jnp.int16),
                pltpu.VMEM((n_layer, RB * BS, LANES), jnp.int16),
                pltpu.VMEM((n_layer, 8, LANES), F32),
                pltpu.VMEM((n_layer, 8, LANES), F32),
                dma((8,)),
                dma((n_col, 2)), dma((n_col, 2)), dma((n_col,)), dma((n_col,)),
                dma((chips, 2)), dma((chips, 2)), dma((chips, 2)), dma((chips, 2)),
                dma, dma,
                dma((n_row,)), dma((n_row,)),
                dma((n_layer,)), dma((n_layer,)), dma((n_layer,)), dma((n_layer,)),
            ],
            compiler_params=pltpu.CompilerParams(
                collective_id=0, has_side_effects=True, vmem_limit_bytes=60 * 2**20
            ),
        )(
            a_vals.reshape(slots, wide), p_vals.reshape(slots, wide),
            a_rows.reshape(1, slots), a_cols.reshape(1, slots), a_count.reshape(1, 1),
            p_rows.reshape(1, slots), p_cols.reshape(1, slots), p_count.reshape(1, 1),
        )
        return got.transpose(1, 0, 2).reshape(RB * BS, LANES)

    placed = (
        P("row", "col", "layer", None, None),
        P("row", "col", "layer", None),
        P("row", "col", "layer", None),
        P("row", "col", "layer"),
    ) * 2
    return jax.shard_map(
        on_device, mesh=mesh, in_specs=placed, out_specs=P("row", ("col", "layer")), check_vma=False
    )
```

profile of v0, /device:TPU:0, one launch (start us, length us, event | category | flops | bytes accessed | tf_op | source)
XLA Modules:
  0.0 30.3 jit_solution(4186299892746668726)
XLA Ops:
  1.3 27.3 %shard_map.82 = f32[64,8,128]{2,1,0:T(8,128)} custom-call(bf16[32,4096]{1,0:T(8,128)(2,1)} %bitcast.13, bf16[32,4096]{1,0:T(8,128)(2,1)} %bitcast.14, s32[1,32]{1,0:T(1,128)} %bitcast.15, s32[1,32]{1,0:T(1,128)} %bitcast.16, s32[1,1]{1,0:T(1,128)} %bitcast.10.rest_2_, s32[1,32]{1,0:T(1,128)} %bitcast.17, s32[1,32]{1,0:T(1,128)} %bitcast.18, ...), custom_call_target="tpu_custom_call" | custom-call | tf_op jit(solution)/shard_map/pallas_call | solution.py:308
  28.6 1.7 %copy.9 = f32[8,64,128]{2,1,0:T(8,128)} copy(f32[8,64,128]{2,0,1:T(8,128)} %bitcast.12) | data formatting | bytes 524288 | tf_op jit(solution)/shard_map/transpose | solution.py:346
where the time goes:
time: 30.5 us; the launch traced here: 30.3 us
  Pallas kernels  27.3 us (90%)
  local copies, waits for them, and re-layouts  1.7 us (6%)
  between operations  1.3 us (4%)
    pallas_call x1, Pallas kernels, on_device(): pl.pallas_call(functools.partial(kernel, n_row, n_col, n_layer), out_shap...  27.3 us
    transpose x1, local copies, waits for them, and re-layouts, on_device(): return got.transpose(1, 0, 2).reshape(RB * BS, LANES)  1.7 us

commit v1 on v0

v1 whole, which is shorter than its diff:
```python
import functools

import jax
import jax.numpy as jnp
from jax import lax
from jax.experimental import pallas as pl
from jax.experimental.pallas import tpu as pltpu
from jax.sharding import PartitionSpec as P

BS = 64
RB = 8
KB = 16
JB = 8
LANES = 128
HALF = BS * BS // 2
MESH = pl.DeviceIdType.MESH
F32 = jnp.float32
BF16 = jnp.bfloat16


def positions(rows, cols, count, width):
    slot = lax.broadcasted_iota(jnp.int32, rows.shape, 1)
    pos = jnp.where(slot < count, rows * width + cols, -1)
    row = jnp.concatenate([pos] * (LANES // pos.shape[1]), axis=1)
    return jnp.broadcast_to(row, (8, LANES))


def pair_onehot(pos, pairs, width, slots):
    shape = (pairs * 8, 2 * slots)
    row = lax.broadcasted_iota(jnp.int32, shape, 0)
    lane = lax.broadcasted_iota(jnp.int32, shape, 1)
    want = (row % 8) * width + 2 * (row // 8) + lane // slots
    return jnp.where(want == pos[0:1, : 2 * slots], 1.0, 0.0).astype(BF16)


def spread(vals, onehot, pairs, store, first=0, last=8):
    slots = vals.shape[0]
    low = lax.broadcasted_iota(jnp.int32, (slots, LANES), 1) < BS

    def body(step, carry):
        v = vals[:, pl.ds(pl.multiple_of(step * 512, 512), 512)].astype(F32)
        parts = []
        for g in range(4):
            a = v[:, g * LANES : (g + 1) * LANES]
            b = pltpu.roll(a, BS, 1)
            parts.append(jnp.concatenate([jnp.where(low, a, 0.0), jnp.where(low, 0.0, b)], axis=0))
            parts.append(jnp.concatenate([jnp.where(low, b, 0.0), jnp.where(low, 0.0, a)], axis=0))
        w = jnp.concatenate(parts, axis=1).astype(BF16)
        d = jnp.dot(onehot, w, preferred_element_type=F32)
        for p in range(pairs):
            rows = [d[p * 8 : (p + 1) * 8, i * LANES : (i + 1) * LANES] for i in range(8)]
            store(step, p, jnp.concatenate(rows, axis=0).astype(BF16))
        return carry

    lax.fori_loop(first, last, body, 0, unroll=True)


def quad_onehot(pos, slots):
    row = lax.broadcasted_iota(jnp.int32, (64, slots), 0)
    want = (row % 8) * JB + ((row // 8) % 2) * 4 + row // 16
    return jnp.where(want == pos[0:1, :slots], 1.0, 0.0).astype(BF16)


def lane_of(shape):
    return lax.broadcasted_iota(jnp.int32, shape, 1)


def four(lane, parts):
    low = jnp.where(lane < 32, parts[0], parts[1])
    high = jnp.where(lane < 96, parts[2], parts[3])
    return jnp.where(lane < 64, low, high)


def split(src, dst):
    slots = src.shape[0]
    first = lane_of((slots, LANES)) % BS < 32
    for t in range(16):
        a = src[:, 256 * t : 256 * t + LANES].astype(F32)
        b = src[:, 256 * t + LANES : 256 * t + 256].astype(F32)
        at = slice(t * LANES, (t + 1) * LANES)
        dst[0, :, at] = jnp.where(first, a, pltpu.roll(b, 32, 1)).astype(BF16)
        dst[1, :, at] = jnp.where(first, pltpu.roll(a, 96, 1), b).astype(BF16)


def spread_half(vals, onehot, store):
    lane = lane_of((8, LANES))
    for step in range(4):
        v = vals[:, step * 512 : (step + 1) * 512].astype(F32)
        parts = []
        for g in range(4):
            a = v[:, g * LANES : (g + 1) * LANES]
            parts += [a] + [pltpu.roll(a, 32 * r, 1) for r in range(1, 4)]
        w = jnp.concatenate(parts, axis=1).astype(BF16)
        d = jnp.dot(onehot, w, preferred_element_type=F32)
        for z in range(2):
            rows = []
            for kin in range(16):
                g, u = kin // 4, (0, 2, 1, 3)[kin % 4]
                at = [(g * 4 + (m - u) % 4) * LANES for m in range(4)]
                rows.append(
                    four(lane, [d[m * 16 + z * 8 : m * 16 + z * 8 + 8, at[m] : at[m] + LANES] for m in range(4)])
                )
            store(step, z, jnp.concatenate(rows, axis=0).astype(BF16))


def kernel(
    n_row, n_col, n_layer, a_hbm, p_hbm, *rest,
):
    small_hbm, out, small, scratch = rest[:6], rest[6], rest[7:13], rest[13:]
    (
    a_buf, p_raw, p_buf, a_pos, p_pos, a_own_pos, p_own_pos, a_dense, a_mixed, p_dense, order, acc, total,
    code, code_in, peak, peak_in,
    loc_sem, a_send, a_recv, ap_send, ap_recv, p_send, p_recv, r_send, r_recv, s_send, s_recv, pp_send, pp_recv,
    c_send, c_recv, m_send, m_recv,
    ) = scratch
    row, col, lay = lax.axis_index("row"), lax.axis_index("col"), lax.axis_index("layer")
    core = lax.rem(row, 2)
    sib = row + 1 - 2 * core
    chips = n_row // 2
    slots = a_hbm.shape[0]

    barrier = pltpu.get_barrier_semaphore()
    for d in range(1, n_row):
        pl.semaphore_signal(barrier, inc=1, device_id={"row": lax.rem(row + d, n_row)}, device_id_type=MESH)
    for d in range(1, n_col):
        pl.semaphore_signal(barrier, inc=1, device_id={"col": lax.rem(col + d, n_col)}, device_id_type=MESH)
    for d in range(1, n_layer):
        pl.semaphore_signal(barrier, inc=1, device_id={"layer": lax.rem(lay + d, n_layer)}, device_id_type=MESH)
    own_a = pltpu.make_async_copy(a_hbm, a_buf.at[0], loc_sem.at[0])
    own_p = pltpu.make_async_copy(p_hbm, p_raw, loc_sem.at[1])
    tables = [pltpu.make_async_copy(small_hbm[k], small[k], loc_sem.at[2 + k]) for k in range(6)]
    own_p.start()
    for copy in tables:
        copy.start()
    own_a.start()

    def remote(src, dst, send, recv, where):
        return pltpu.make_async_remote_copy(
            src_ref=src, dst_ref=dst, send_sem=send, recv_sem=recv, device_id=where, device_id_type=MESH
        )

    def piece(ref, h):
        return ref.at[:, pl.ds(h * HALF, HALF)]

    across, relay, over, over_marks, marks = {}, {}, {}, {}, []
    for h in range(2):
        for d in range(1, chips):
            to = {"row": lax.rem(row + 2 * d, n_row)}
            across[d, h] = remote(p_buf.at[0, h], p_buf.at[2 * d, h], p_send.at[d, h], p_recv.at[d, h], to)
            relay[d, h] = remote(
                p_buf.at[2 * d, h], p_buf.at[2 * d + 1, h], r_send.at[d, h], r_recv.at[d, h], {"row": sib}
            )
        for d in range(1, n_col):
            to = {"col": lax.rem(col + d, n_col)}
            over[d, h] = remote(piece(a_hbm, h), piece(a_buf.at[d], h), a_send.at[d, h], a_recv.at[d, h], to)
    for d in range(1, n_col):
        to = {"col": lax.rem(col + d, n_col)}
        over_marks[d] = remote(a_own_pos, a_pos.at[d], ap_send.at[d], ap_recv.at[d], to)
    for d in range(1, n_row):
        to = lax.rem(row + d, n_row) if d % 2 == 0 else lax.rem(sib + d - 1, n_row)
        marks.append(remote(p_own_pos, p_pos.at[d], pp_send.at[d], pp_recv.at[d], {"row": to}))
    beside = remote(p_buf.at[0], p_buf.at[1], s_send, s_recv, {"row": sib})

    own_p.wait()
    split(p_raw, p_buf.at[0])
    for copy in tables:
        copy.wait()
    a_rows, a_cols, a_count, p_rows, p_cols, p_count = small
    a_own_pos[...] = positions(a_rows[...], a_cols[...], a_count[...], KB)
    p_own_pos[...] = positions(p_rows[...], p_cols[...], p_count[...], JB)
    pl.semaphore_wait(barrier, n_row + n_col + n_layer - 3)
    for h in range(2):
        for d in range(1, chips):
            across[d, h].start()
        for d in range(1, n_col):
            over[d, h].start()
        if h == 0:
            for copy in marks + list(over_marks.values()) + [beside]:
                copy.start()

    shape = order.shape
    r = lax.broadcasted_iota(jnp.int32, shape, 0)
    c = lax.broadcasted_iota(jnp.int32, shape, 1)
    order[...] = jnp.where(c == (r % BS) * 8 + r // BS, 1.0, 0.0).astype(BF16)

    def take_a(d, h):
        pos = a_own_pos if d == 0 else a_pos.at[d]
        onehot = pair_onehot(pos[...], KB // 2, KB, slots)
        first = 2 * lax.rem(col - d + n_col, n_col)

        def store(step, p, rows):
            lanes = pl.ds((p % 4) * LANES, LANES)
            a_mixed[p // 4, pl.ds(pl.multiple_of(step * 64, 64), 64), lanes] = rows

        spread(a_buf.at[d], onehot, KB // 2, store, 4 * h, 4 * h + 4)
        rows = pl.ds(h * 256, 256)
        for q in range(2):
            a_dense[first + q, rows, :] = jnp.dot(
                a_mixed[q, rows, :], order[...], preferred_element_type=F32
            ).astype(BF16)

    def take_p(d, h):
        pos = p_own_pos if d == 0 else p_pos.at[d]

        def store(step, z, rows):
            p_dense[h, d, step * LANES : (step + 1) * LANES, z * LANES : (z + 1) * LANES] = rows

        spread_half(p_buf.at[d, h], quad_onehot(pos[...], slots), store)

    def source(d):
        base = row if d % 2 == 0 else sib
        return lax.rem(base - 2 * (d // 2) + n_row, n_row)

    inner = jnp.logical_or(lay == 1, lay == 2)
    near = lay + 1 - 2 * lax.rem(lay, 2)
    far = lax.rem(lay + 2, 4)
    opposite = 3 - lay
    lane = lane_of((LANES, LANES))

    def multiply(rh, ch):
        rows = pl.ds(rh * 256, 256)
        k = 2 * ch + rh
        sum_ = jnp.dot(a_dense[source(0), rows, :], p_dense[ch, 0], preferred_element_type=F32)
        for d in range(1, n_row):
            sum_ += jnp.dot(a_dense[source(d), rows, :], p_dense[ch, d], preferred_element_type=F32)
        acc[k] = sum_

    def packed(k, to):
        lanes = pl.ds(pl.multiple_of((to // 2) * LANES, LANES), LANES)
        x, y = acc[k, 0:LANES, lanes], acc[k, LANES : 2 * LANES, lanes]
        odd = lax.rem(to, 2)
        stays = jnp.where(odd == 0, x, y)
        moves = pltpu.roll(jnp.where(odd == 0, y, x), BS, 1)
        return jnp.where(lane // BS == odd, stays, moves)

    def encode(k, j, x):
        top = jnp.maximum(jnp.max(jnp.abs(x), axis=0, keepdims=True), 1.2e-38)
        peak[k, j] = top
        q = jnp.round((x * (1.0 / top)) * 32767.0)
        code[k, j] = q.astype(jnp.int32).astype(jnp.int16)

    def decode(k, j):
        q = code_in[k, j].astype(jnp.int32).astype(F32)
        return (q * (1.0 / 32767.0)) * peak_in[k, j]

    def hand(k, j, slot, to):
        where = {"layer": to}
        return (
            remote(code.at[k, j], code_in.at[k, slot], c_send.at[k, j], c_recv.at[k, slot], where),
            remote(peak.at[k, j], peak_in.at[k, slot], m_send.at[k, j], m_recv.at[k, slot], where),
        )

    def via(k):
        return hand(k, 0, jnp.where(inner, 3, 0), jnp.where(inner, opposite, near))

    def start(copies):
        for copy in copies:
            copy.start()

    def arrive(copies):
        for copy in copies:
            copy.wait_recv()

    def launch(k):
        encode(k, 0, packed(k, opposite))
        start(via(k))

        @pl.when(jnp.logical_not(inner))
        def _():
            encode(k, 2, packed(k, far))
            start(hand(k, 2, 2, far))

        encode(k, 1, packed(k, near))
        start(hand(k, 1, 1, near))
        total[k] = packed(k, lay)

    def forward(k):
        @pl.when(inner)
        def _():
            arrive(hand(k, 0, 0, near))
            encode(k, 2, packed(k, far) + decode(k, 0))
            start(hand(k, 2, 2, far))

    def collect(k):
        @pl.when(inner)
        def _():
            arrive(hand(k, 0, 3, opposite))
            total[k] += decode(k, 3)

        arrive(hand(k, 1, 1, near))
        x = total[k] + decode(k, 1)
        arrive(hand(k, 2, 2, far))
        return x + decode(k, 2)

    take_p(0, 0)
    own_a.wait()
    take_a(0, 0)
    beside.wait_recv()
    marks[0].wait_recv()
    take_p(1, 0)
    take_a(0, 1)
    take_p(0, 1)
    take_p(1, 1)
    for d in range(1, chips):
        across[d, 0].wait_recv()
        relay[d, 0].start()
    for d in range(1, n_col):
        over_marks[d].wait_recv()
        over[d, 0].wait_recv()
        take_a(d, 0)
    for d in range(2, n_row):
        marks[d - 1].wait_recv()
        if d % 2:
            relay[d // 2, 0].wait_recv()
        take_p(d, 0)
    multiply(0, 0)
    launch(0)
    for d in range(1, chips):
        across[d, 1].wait_recv()
        relay[d, 1].start()
    for d in range(1, n_col):
        over[d, 1].wait_recv()
        take_a(d, 1)
    multiply(1, 0)
    launch(1)
    forward(0)
    for d in range(2, n_row):
        if d % 2:
            relay[d // 2, 1].wait_recv()
        take_p(d, 1)
    multiply(0, 1)
    launch(2)
    multiply(1, 1)
    launch(3)
    for k in range(1, 4):
        forward(k)
    for rh in range(2):
        f, g = collect(rh), collect(2 + rh)
        for s in range(2):
            if s == 0:
                x = four(lane, [f, pltpu.roll(g, 32, 1), pltpu.roll(f, 32, 1), pltpu.roll(g, 64, 1)])
            else:
                x = four(lane, [pltpu.roll(f, 64, 1), pltpu.roll(g, 96, 1), pltpu.roll(f, 96, 1), g])
            out[pl.ds(rh * 32 + s * 16, 16)] = x.reshape(16, 8, LANES)

    sums = []
    for k in range(4):
        sums += list(via(k)) + list(hand(k, 2, 2, far)) + list(hand(k, 1, 1, near))
    for copy in list(across.values()) + list(relay.values()) + list(over.values()) + list(over_marks.values()):
        copy.wait_send()
    for copy in marks + sums + [beside]:
        copy.wait_send()


def solution(mesh):
    n_row, n_col, n_layer = (mesh.shape[k] for k in ("row", "col", "layer"))

    def on_device(a_vals, a_rows, a_cols, a_count, p_vals, p_rows, p_cols, p_count):
        slots = a_vals.shape[3]
        wide = BS * BS
        any_space = pl.BlockSpec(memory_space=pltpu.HBM)
        vmem = pl.BlockSpec(memory_space=pltpu.VMEM)
        dma = pltpu.SemaphoreType.DMA
        chips = n_row // 2
        got = pl.pallas_call(
            functools.partial(kernel, n_row, n_col, n_layer),
            out_shape=jax.ShapeDtypeStruct((BS, RB, LANES), F32),
            in_specs=[any_space] * 8,
            out_specs=vmem,
            scratch_shapes=(
                [pltpu.VMEM((1, slots), jnp.int32)] * 2 + [pltpu.VMEM((1, 1), jnp.int32)]
            ) * 2 + [
                pltpu.VMEM((n_col, slots, wide), BF16),
                pltpu.VMEM((slots, wide), BF16),
                pltpu.VMEM((n_row, 2, slots, HALF), BF16),
                pltpu.VMEM((n_col, 8, LANES), jnp.int32),
                pltpu.VMEM((n_row, 8, LANES), jnp.int32),
                pltpu.VMEM((8, LANES), jnp.int32),
                pltpu.VMEM((8, LANES), jnp.int32),
                pltpu.VMEM((n_row, RB * BS, 8 * BS), BF16),
                pltpu.VMEM((2, RB * BS, 8 * BS), BF16),
                pltpu.VMEM((2, n_row, 8 * BS, JB * BS // 2), BF16),
                pltpu.VMEM((8 * BS, 8 * BS), BF16),
                pltpu.VMEM((4, 256, 256), F32),
                pltpu.VMEM((4, LANES, LANES), F32),
                pltpu.VMEM((4, 3, LANES, LANES), jnp.int16),
                pltpu.VMEM((4, 4, LANES, LANES), jnp.int16),
                pltpu.VMEM((4, 3, 1, LANES), F32),
                pltpu.VMEM((4, 4, 1, LANES), F32),
                dma((8,)),
                dma((n_col, 2)), dma((n_col, 2)), dma((n_col,)), dma((n_col,)),
                dma((chips, 2)), dma((chips, 2)), dma((chips, 2)), dma((chips, 2)),
                dma, dma,
                dma((n_row,)), dma((n_row,)),
                dma((4, 3)), dma((4, 4)), dma((4, 3)), dma((4, 4)),
            ],
            compiler_params=pltpu.CompilerParams(
                collective_id=0, has_side_effects=True, vmem_limit_bytes=56_200_000
            ),
        )(
            a_vals.reshape(slots, wide), p_vals.reshape(slots, wide),
            a_rows.reshape(1, slots), a_cols.reshape(1, slots), a_count.reshape(1, 1),
            p_rows.reshape(1, slots), p_cols.reshape(1, slots), p_count.reshape(1, 1),
        )
        return got.transpose(1, 0, 2).reshape(RB * BS, LANES)

    placed = (
        P("row", "col", "layer", None, None),
        P("row", "col", "layer", None),
        P("row", "col", "layer", None),
        P("row", "col", "layer"),
    ) * 2
    return jax.shard_map(
        on_device, mesh=mesh, in_specs=placed, out_specs=P("row", ("col", "layer")), check_vma=False
    )
```

time: 30.5 us -> 30.2 us (level)
    transpose x1, local copies, waits for them, and re-layouts: 1.7 us -> 0.75 us  [on_device(): return got.transpose(1, 0, 2).reshape(RB * BS, LANES)]
    unnamed x0 -> x8, local copies, waits for them, and re-layouts: none -> 0.67 us
where the time goes in v1:
time: 30.2 us; the launch traced here: 30.1 us
  Pallas kernels  27.3 us (90%)
  local copies, waits for them, and re-layouts  1.42 us (5%)
  between operations  1.34 us (4%)
    pallas_call x1, Pallas kernels, on_device(): pl.pallas_call(functools.partial(kernel, n_row, n_col, n_layer), out_shap...  27.3 us
    transpose x1, local copies, waits for them, and re-layouts, on_device(): return got.transpose(1, 0, 2).reshape(RB * BS, LANES)  0.75 us
    unnamed x8, local copies, waits for them, and re-layouts  0.67 us

profile of v1, /device:TPU:0, one launch (start us, length us, event | category | flops | bytes accessed | tf_op | source)
XLA Modules:
  0.0 30.1 jit_solution(17251347827845814060)
XLA Ops:
  1.3 0.0 copy-start.3
  1.3 0.0 copy-start
  1.3 0.0 copy-start.1
  1.3 0.0 copy-start.2
  1.3 0.6 %copy-done.3 = s32[1,1,1,32]{3,2,1,0:T(1,128)S(1)} copy-done((s32[1,1,1,32]{3,2,1,0:T(1,128)S(1)}, s32[1,1,1,32]{3,2,1,0:T(1,128)}, u32[]{:S(2)}) %copy-start.3) | copy-done | bytes 152
  2.0 0.0 copy-done
  2.0 0.0 copy-done.1
  2.0 0.0 copy-done.2
  2.0 27.3 %shard_map.82 = f32[64,8,128]{2,1,0:T(8,128)S(1)} custom-call(bf16[32,4096]{1,0:T(8,128)(2,1)} %bitcast.17, bf16[32,4096]{1,0:T(8,128)(2,1)} %bitcast.18, s32[1,32]{1,0:T(1,128)S(1)} %bitcast.13, s32[1,32]{1,0:T(1,128)S(1)} %bitcast.14, s32[1,1]{1,0:T(1,128)} %bitcast.10.rest_2_, s32[1,32]{1,0:T(1,128)S(1)} %bitcast.15, s32[1,32]{1,0:T(1,128)S(1)} %bitcast.16, ...), custom_call_target="tpu_custom_call" | custom-call | tf_op jit(solution)/shard_map/pallas_call | solution.py:365
  29.3 0.8 %copy.9 = f32[8,64,128]{2,1,0:T(8,128)} copy(f32[8,64,128]{2,0,1:T(8,128)S(1)} %bitcast.12) | data formatting | bytes 524288 | tf_op jit(solution)/shard_map/transpose | solution.py:405
Async XLA Ops:
  1.3 0.7 %copy-start.3 = (s32[1,1,1,32]{3,2,1,0:T(1,128)S(1)}, s32[1,1,1,32]{3,2,1,0:T(1,128)}, u32[]{:S(2)}) copy-start(s32[1,1,1,32]{3,2,1,0:T(1,128)} %param.14) | copy-start | bytes 388
  1.3 0.7 %copy-start = (s32[1,1,1,32]{3,2,1,0:T(1,128)S(1)}, s32[1,1,1,32]{3,2,1,0:T(1,128)}, u32[]{:S(2)}) copy-start(s32[1,1,1,32]{3,2,1,0:T(1,128)} %param.9) | copy-start | bytes 388
  1.3 0.7 %copy-start.1 = (s32[1,1,1,32]{3,2,1,0:T(1,128)S(1)}, s32[1,1,1,32]{3,2,1,0:T(1,128)}, u32[]{:S(2)}) copy-start(s32[1,1,1,32]{3,2,1,0:T(1,128)} %param.10) | copy-start | bytes 388
  1.3 0.7 %copy-start.2 = (s32[1,1,1,32]{3,2,1,0:T(1,128)S(1)}, s32[1,1,1,32]{3,2,1,0:T(1,128)}, u32[]{:S(2)}) copy-start(s32[1,1,1,32]{3,2,1,0:T(1,128)} %param.13) | copy-start | bytes 388

commit v2 on v0

--- a/solution.py
+++ b/solution.py
@@ -57,7 +57,7 @@
 def kernel(
     n_row, n_col, n_layer, a_hbm, p_hbm, *rest,
 ):
-    small_hbm, out, small, scratch = rest[:6], rest[6], rest[7:13], rest[13:]
+    small_hbm, (a_count, p_count), out, small, scratch = rest[:4], rest[4:6], rest[6], rest[7:11], rest[11:]
     (
     a_buf, p_buf, a_pos, p_pos, a_own_pos, p_own_pos, a_dense, a_mixed, p_dense, order, acc, code, code_in, peak, peak_in,
     loc_sem, a_send, a_recv, ap_send, ap_recv, p_send, p_recv, r_send, r_recv, s_send, s_recv, pp_send, pp_recv,
@@ -72,7 +72,7 @@
 
     own_a = pltpu.make_async_copy(a_hbm, a_buf.at[0], loc_sem.at[0])
     own_p = pltpu.make_async_copy(p_hbm, p_buf.at[0], loc_sem.at[1])
-    tables = [pltpu.make_async_copy(small_hbm[k], small[k], loc_sem.at[2 + k]) for k in range(6)]
+    tables = [pltpu.make_async_copy(small_hbm[k], small[k], loc_sem.at[2 + k]) for k in range(4)]
     for copy in tables:
         copy.start()
     own_p.start()
@@ -115,9 +115,9 @@
                 over[d, h].start()
     for copy in tables:
         copy.wait()
-    a_rows, a_cols, a_count, p_rows, p_cols, p_count = small
-    a_own_pos[...] = positions(a_rows[...], a_cols[...], a_count[...], KB)
-    p_own_pos[...] = positions(p_rows[...], p_cols[...], p_count[...], JB)
+    a_rows, a_cols, p_rows, p_cols = small
+    a_own_pos[...] = positions(a_rows[...], a_cols[...], a_count[0, 0], KB)
+    p_own_pos[...] = positions(p_rows[...], p_cols[...], p_count[0, 0], JB)
     over_marks = {}
     for d in range(1, n_col):
         to = {"col": lax.rem(col + d, n_col)}
@@ -303,16 +303,21 @@
         wide = BS * BS
         any_space = pl.BlockSpec(memory_space=pltpu.HBM)
         vmem = pl.BlockSpec(memory_space=pltpu.VMEM)
+        scalar = pl.BlockSpec(memory_space=pltpu.SMEM)
+
+        def keep(x, shape):
+            return pltpu.with_memory_space_constraint(x.reshape(shape), pltpu.HBM)
+
         dma = pltpu.SemaphoreType.DMA
         chips = n_row // 2
         got = pl.pallas_call(
             functools.partial(kernel, n_row, n_col, n_layer),
             out_shape=jax.ShapeDtypeStruct((BS, RB, LANES), F32),
-            in_specs=[any_space] * 8,
+            in_specs=[any_space] * 6 + [scalar] * 2,
             out_specs=vmem,
             scratch_shapes=(
-                [pltpu.VMEM((1, slots), jnp.int32)] * 2 + [pltpu.VMEM((1, 1), jnp.int32)]
-            ) * 2 + [
+                [pltpu.VMEM((1, slots), jnp.int32)] * 4
+            ) + [
                 pltpu.VMEM((n_col, slots, wide), BF16),
                 pltpu.VMEM((n_row, slots, wide), BF16),
                 pltpu.VMEM((n_col, 8, LANES), jnp.int32),
@@ -336,12 +341,11 @@
                 dma((n_layer,)), dma((n_layer,)), dma((n_layer,)), dma((n_layer,)),
             ],
             compiler_params=pltpu.CompilerParams(
-                collective_id=0, has_side_effects=True, vmem_limit_bytes=60 * 2**20
+                collective_id=0, has_side_effects=True, vmem_limit_bytes=40 * 2**20
             ),
         )(
-            a_vals.reshape(slots, wide), p_vals.reshape(slots, wide),
-            a_rows.reshape(1, slots), a_cols.reshape(1, slots), a_count.reshape(1, 1),
-            p_rows.reshape(1, slots), p_cols.reshape(1, slots), p_count.reshape(1, 1),
+            keep(a_vals, (slots, wide)), keep(p_vals, (slots, wide)), keep(a_rows, (1, slots)), keep(a_cols, (1, slots)),
+            keep(p_rows, (1, slots)), keep(p_cols, (1, slots)), a_count.reshape(1, 1), p_count.reshape(1, 1),
         )
         return got.transpose(1, 0, 2).reshape(RB * BS, LANES)
 

time: 30.5 us -> 28.8 us (0.944)
  local copies, waits for them, and re-layouts: 1.7 us -> 0.75 us
  Pallas kernels: 27.3 us -> 26.6 us
    transpose x1, local copies, waits for them, and re-layouts: 1.7 us -> 0.75 us  [on_device(): return got.transpose(1, 0, 2).reshape(RB * BS, LANES)]
    pallas_call x1, Pallas kernels: 27.3 us -> 26.6 us  [on_device(): pl.pallas_call(functools.partial(kernel, n_row, n_col, n_layer), out_shap...]
where the time goes in v2:
time: 28.8 us; the launch traced here: 28.7 us
  Pallas kernels  26.6 us (92%)
  between operations  1.3 us (5%)
  local copies, waits for them, and re-layouts  0.75 us (3%)
    pallas_call x1, Pallas kernels, on_device(): pl.pallas_call(functools.partial(kernel, n_row, n_col, n_layer), out_shap...  26.6 us
    transpose x1, local copies, waits for them, and re-layouts, on_device(): return got.transpose(1, 0, 2).reshape(RB * BS, LANES)  0.75 us

profile of v2, /device:TPU:0, one launch (start us, length us, event | category | flops | bytes accessed | tf_op | source)
XLA Modules:
  0.0 28.7 jit_solution(11165502058674795211)
XLA Ops:
  1.3 26.6 %shard_map.82 = f32[64,8,128]{2,1,0:T(8,128)S(1)} custom-call(bf16[32,4096]{1,0:T(8,128)(2,1)} %bitcast.13, bf16[32,4096]{1,0:T(8,128)(2,1)} %bitcast.14, s32[1,32]{1,0:T(1,128)} %bitcast.15, s32[1,32]{1,0:T(1,128)} %bitcast.16, s32[1,32]{1,0:T(1,128)} %bitcast.17, s32[1,32]{1,0:T(1,128)} %bitcast.18, s32[1,1]{1,0:T(1,128)} %bitcast.10.rest_4_, ...), custom_call_target="tpu_custom_call" | custom-call | tf_op jit(solution)/shard_map/pallas_call | solution.py:313
  27.9 0.8 %copy.9 = f32[8,64,128]{2,1,0:T(8,128)} copy(f32[8,64,128]{2,0,1:T(8,128)S(1)} %bitcast.12) | data formatting | bytes 524288 | tf_op jit(solution)/shard_map/transpose | solution.py:350

commit v3 on v1

--- a/solution.py
+++ b/solution.py
@@ -106,11 +106,11 @@
 def kernel(
     n_row, n_col, n_layer, a_hbm, p_hbm, *rest,
 ):
-    small_hbm, out, small, scratch = rest[:6], rest[6], rest[7:13], rest[13:]
+    small_hbm, (a_count, p_count), out, small, scratch = rest[:4], rest[4:6], rest[6], rest[7:11], rest[11:]
     (
     a_buf, p_raw, p_buf, a_pos, p_pos, a_own_pos, p_own_pos, a_dense, a_mixed, p_dense, order, acc, total,
     code, code_in, peak, peak_in,
-    loc_sem, a_send, a_recv, ap_send, ap_recv, p_send, p_recv, r_send, r_recv, s_send, s_recv, pp_send, pp_recv,
+    loc_sem, a_send, a_recv, ap_send, ap_recv, p_send, p_recv, r_send, r_recv, pp_send, pp_recv,
     c_send, c_recv, m_send, m_recv,
     ) = scratch
     row, col, lay = lax.axis_index("row"), lax.axis_index("col"), lax.axis_index("layer")
@@ -128,7 +128,7 @@
         pl.semaphore_signal(barrier, inc=1, device_id={"layer": lax.rem(lay + d, n_layer)}, device_id_type=MESH)
     own_a = pltpu.make_async_copy(a_hbm, a_buf.at[0], loc_sem.at[0])
     own_p = pltpu.make_async_copy(p_hbm, p_raw, loc_sem.at[1])
-    tables = [pltpu.make_async_copy(small_hbm[k], small[k], loc_sem.at[2 + k]) for k in range(6)]
+    tables = [pltpu.make_async_copy(small_hbm[k], small[k], loc_sem.at[2 + k]) for k in range(4)]
     own_p.start()
     for copy in tables:
         copy.start()
@@ -142,32 +142,31 @@
     def piece(ref, h):
         return ref.at[:, pl.ds(h * HALF, HALF)]
 
-    across, relay, over, over_marks, marks = {}, {}, {}, {}, []
+    across, shared, over, over_marks, marks = {}, {}, {}, {}, []
     for h in range(2):
-        for d in range(1, chips):
+        for d in range(chips):
             to = {"row": lax.rem(row + 2 * d, n_row)}
-            across[d, h] = remote(p_buf.at[0, h], p_buf.at[2 * d, h], p_send.at[d, h], p_recv.at[d, h], to)
-            relay[d, h] = remote(
-                p_buf.at[2 * d, h], p_buf.at[2 * d + 1, h], r_send.at[d, h], r_recv.at[d, h], {"row": sib}
-            )
+            if d:
+                across[d, h] = remote(p_buf.at[0, h], p_buf.at[d, h], p_send.at[d, h], p_recv.at[d, h], to)
+            mine, theirs = p_dense.at[h, 2 * d], p_dense.at[h, 2 * d + 1]
+            shared[d, h] = remote(mine, theirs, r_send.at[d, h], r_recv.at[d, h], {"row": sib})
         for d in range(1, n_col):
             to = {"col": lax.rem(col + d, n_col)}
             over[d, h] = remote(piece(a_hbm, h), piece(a_buf.at[d], h), a_send.at[d, h], a_recv.at[d, h], to)
     for d in range(1, n_col):
         to = {"col": lax.rem(col + d, n_col)}
         over_marks[d] = remote(a_own_pos, a_pos.at[d], ap_send.at[d], ap_recv.at[d], to)
-    for d in range(1, n_row):
-        to = lax.rem(row + d, n_row) if d % 2 == 0 else lax.rem(sib + d - 1, n_row)
-        marks.append(remote(p_own_pos, p_pos.at[d], pp_send.at[d], pp_recv.at[d], {"row": to}))
-    beside = remote(p_buf.at[0], p_buf.at[1], s_send, s_recv, {"row": sib})
+    for d in range(1, chips):
+        to = {"row": lax.rem(row + 2 * d, n_row)}
+        marks.append(remote(p_own_pos, p_pos.at[d], pp_send.at[d], pp_recv.at[d], to))
 
     own_p.wait()
     split(p_raw, p_buf.at[0])
     for copy in tables:
         copy.wait()
-    a_rows, a_cols, a_count, p_rows, p_cols, p_count = small
-    a_own_pos[...] = positions(a_rows[...], a_cols[...], a_count[...], KB)
-    p_own_pos[...] = positions(p_rows[...], p_cols[...], p_count[...], JB)
+    a_rows, a_cols, p_rows, p_cols = small
+    a_own_pos[...] = positions(a_rows[...], a_cols[...], a_count[0, 0], KB)
+    p_own_pos[...] = positions(p_rows[...], p_cols[...], p_count[0, 0], JB)
     pl.semaphore_wait(barrier, n_row + n_col + n_layer - 3)
     for h in range(2):
         for d in range(1, chips):
@@ -175,7 +174,7 @@
         for d in range(1, n_col):
             over[d, h].start()
         if h == 0:
-            for copy in marks + list(over_marks.values()) + [beside]:
+            for copy in marks + list(over_marks.values()):
                 copy.start()
 
     shape = order.shape
@@ -203,9 +202,10 @@
         pos = p_own_pos if d == 0 else p_pos.at[d]
 
         def store(step, z, rows):
-            p_dense[h, d, step * LANES : (step + 1) * LANES, z * LANES : (z + 1) * LANES] = rows
+            p_dense[h, 2 * d, step * LANES : (step + 1) * LANES, z * LANES : (z + 1) * LANES] = rows
 
         spread_half(p_buf.at[d, h], quad_onehot(pos[...], slots), store)
+        shared[d, h].start()
 
     def source(d):
         base = row if d % 2 == 0 else sib
@@ -217,13 +217,12 @@
     opposite = 3 - lay
     lane = lane_of((LANES, LANES))
 
-    def multiply(rh, ch):
-        rows = pl.ds(rh * 256, 256)
-        k = 2 * ch + rh
-        sum_ = jnp.dot(a_dense[source(0), rows, :], p_dense[ch, 0], preferred_element_type=F32)
+    def multiply(first, ch, rows):
+        total_ = jnp.dot(a_dense[source(0), rows, :], p_dense[ch, 0], preferred_element_type=F32)
         for d in range(1, n_row):
-            sum_ += jnp.dot(a_dense[source(d), rows, :], p_dense[ch, d], preferred_element_type=F32)
-        acc[k] = sum_
+            total_ += jnp.dot(a_dense[source(d), rows, :], p_dense[ch, d], preferred_element_type=F32)
+        for k in range(total_.shape[0] // 256):
+            acc[first + k] = total_[k * 256 : (k + 1) * 256]
 
     def packed(k, to):
         lanes = pl.ds(pl.multiple_of((to // 2) * LANES, LANES), LANES)
@@ -235,23 +234,25 @@
 
     def encode(k, j, x):
         top = jnp.maximum(jnp.max(jnp.abs(x), axis=0, keepdims=True), 1.2e-38)
-        peak[k, j] = top
+        peak[j, k] = top
         q = jnp.round((x * (1.0 / top)) * 32767.0)
-        code[k, j] = q.astype(jnp.int32).astype(jnp.int16)
-
-    def decode(k, j):
-        q = code_in[k, j].astype(jnp.int32).astype(F32)
-        return (q * (1.0 / 32767.0)) * peak_in[k, j]
-
-    def hand(k, j, slot, to):
-        where = {"layer": to}
+        code[j, k] = q.astype(jnp.int32).astype(jnp.int16)
+
+    def decode(k, slot):
+        q = code_in[slot, k].astype(jnp.int32).astype(F32)
+        return (q * (1.0 / 32767.0)) * peak_in[slot, k]
+
+    groups = ((0,), (1,), (2, 3))
+
+    def hand(g, j, slot, to):
+        where, ks = {"layer": to}, pl.ds(groups[g][0], len(groups[g]))
         return (
-            remote(code.at[k, j], code_in.at[k, slot], c_send.at[k, j], c_recv.at[k, slot], where),
-            remote(peak.at[k, j], peak_in.at[k, slot], m_send.at[k, j], m_recv.at[k, slot], where),
+            remote(code.at[j, ks], code_in.at[slot, ks], c_send.at[g, j], c_recv.at[g, slot], where),
+            remote(peak.at[j, ks], peak_in.at[slot, ks], m_send.at[g, j], m_recv.at[g, slot], where),
         )
 
-    def via(k):
-        return hand(k, 0, jnp.where(inner, 3, 0), jnp.where(inner, opposite, near))
+    def via(g):
+        return hand(g, 0, jnp.where(inner, 3, 0), jnp.where(inner, opposite, near))
 
     def start(copies):
         for copy in copies:
@@ -261,81 +262,85 @@
         for copy in copies:
             copy.wait_recv()
 
-    def launch(k):
-        encode(k, 0, packed(k, opposite))
-        start(via(k))
+    def ready(g):
+        for k in groups[g]:
+            encode(k, 0, packed(k, opposite))
+        start(via(g))
 
         @pl.when(jnp.logical_not(inner))
         def _():
-            encode(k, 2, packed(k, far))
-            start(hand(k, 2, 2, far))
-
-        encode(k, 1, packed(k, near))
-        start(hand(k, 1, 1, near))
-        total[k] = packed(k, lay)
-
-    def forward(k):
+            for k in groups[g]:
+                encode(k, 2, packed(k, far))
+            start(hand(g, 2, 2, far))
+
+        for k in groups[g]:
+            encode(k, 1, packed(k, near))
+            total[k] = packed(k, lay)
+
+    def send_near(g):
+        start(hand(g, 1, 1, near))
+
+    def forward(g):
         @pl.when(inner)
         def _():
-            arrive(hand(k, 0, 0, near))
-            encode(k, 2, packed(k, far) + decode(k, 0))
-            start(hand(k, 2, 2, far))
-
-    def collect(k):
+            arrive(hand(g, 0, 0, near))
+            for k in groups[g]:
+                encode(k, 2, packed(k, far) + decode(k, 0))
+            start(hand(g, 2, 2, far))
+
+    def collect(g):
         @pl.when(inner)
         def _():
-            arrive(hand(k, 0, 3, opposite))
-            total[k] += decode(k, 3)
-
-        arrive(hand(k, 1, 1, near))
-        x = total[k] + decode(k, 1)
-        arrive(hand(k, 2, 2, far))
-        return x + decode(k, 2)
-
+            arrive(hand(g, 0, 3, opposite))
+            for k in groups[g]:
+                total[k] += decode(k, 3)
+
+        arrive(hand(g, 1, 1, near))
+        for k in groups[g]:
+            total[k] += decode(k, 1)
+        arrive(hand(g, 2, 2, far))
+        for k in groups[g]:
+            total[k] += decode(k, 2)
+
+    def fill(h):
+        for d in range(1, chips):
+            if h == 0:
+                marks[d - 1].wait_recv()
+            across[d, h].wait_recv()
+            take_p(d, h)
+        for d in range(1, n_col):
+            if h == 0:
+                over_marks[d].wait_recv()
+            over[d, h].wait_recv()
+            take_a(d, h)
+
+    own_a.wait()
     take_p(0, 0)
-    own_a.wait()
     take_a(0, 0)
-    beside.wait_recv()
-    marks[0].wait_recv()
-    take_p(1, 0)
+    take_p(0, 1)
     take_a(0, 1)
-    take_p(0, 1)
-    take_p(1, 1)
-    for d in range(1, chips):
-        across[d, 0].wait_recv()
-        relay[d, 0].start()
-    for d in range(1, n_col):
-        over_marks[d].wait_recv()
-        over[d, 0].wait_recv()
-        take_a(d, 0)
-    for d in range(2, n_row):
-        marks[d - 1].wait_recv()
-        if d % 2:
-            relay[d // 2, 0].wait_recv()
-        take_p(d, 0)
-    multiply(0, 0)
-    launch(0)
-    for d in range(1, chips):
-        across[d, 1].wait_recv()
-        relay[d, 1].start()
-    for d in range(1, n_col):
-        over[d, 1].wait_recv()
-        take_a(d, 1)
-    multiply(1, 0)
-    launch(1)
+    fill(0)
+    for d in range(chips):
+        shared[d, 0].wait_recv()
+    multiply(0, 0, pl.ds(0, 256))
+    ready(0)
+    send_near(0)
+    fill(1)
+    multiply(1, 0, pl.ds(256, 256))
+    ready(1)
     forward(0)
-    for d in range(2, n_row):
-        if d % 2:
-            relay[d // 2, 1].wait_recv()
-        take_p(d, 1)
-    multiply(0, 1)
-    launch(2)
-    multiply(1, 1)
-    launch(3)
-    for k in range(1, 4):
-        forward(k)
+    for d in range(chips):
+        shared[d, 1].wait_recv()
+    multiply(2, 1, pl.ds(0, 512))
+    ready(2)
+    send_near(1)
+    forward(1)
+    send_near(2)
+    forward(2)
+    for g in range(3):
+        collect(g)
     for rh in range(2):
-        f, g = collect(rh), collect(2 + rh)
+        f, g = total[rh], total[2 + rh]
         for s in range(2):
             if s == 0:
                 x = four(lane, [f, pltpu.roll(g, 32, 1), pltpu.roll(f, 32, 1), pltpu.roll(g, 64, 1)])
@@ -344,11 +349,11 @@
             out[pl.ds(rh * 32 + s * 16, 16)] = x.reshape(16, 8, LANES)
 
     sums = []
-    for k in range(4):
-        sums += list(via(k)) + list(hand(k, 2, 2, far)) + list(hand(k, 1, 1, near))
-    for copy in list(across.values()) + list(relay.values()) + list(over.values()) + list(over_marks.values()):
+    for g in range(3):
+        sums += list(via(g)) + list(hand(g, 2, 2, far)) + list(hand(g, 1, 1, near))
+    for copy in list(across.values()) + list(shared.values()) + list(over.values()) + list(over_marks.values()):
         copy.wait_send()
-    for copy in marks + sums + [beside]:
+    for copy in marks + sums:
         copy.wait_send()
 
 
@@ -360,21 +365,26 @@
         wide = BS * BS
         any_space = pl.BlockSpec(memory_space=pltpu.HBM)
         vmem = pl.BlockSpec(memory_space=pltpu.VMEM)
+        scalar = pl.BlockSpec(memory_space=pltpu.SMEM)
+
+        def keep(x, shape):
+            return pltpu.with_memory_space_constraint(x.reshape(shape), pltpu.HBM)
+
         dma = pltpu.SemaphoreType.DMA
         chips = n_row // 2
         got = pl.pallas_call(
             functools.partial(kernel, n_row, n_col, n_layer),
             out_shape=jax.ShapeDtypeStruct((BS, RB, LANES), F32),
-            in_specs=[any_space] * 8,
+            in_specs=[any_space] * 6 + [scalar] * 2,
             out_specs=vmem,
             scratch_shapes=(
-                [pltpu.VMEM((1, slots), jnp.int32)] * 2 + [pltpu.VMEM((1, 1), jnp.int32)]
-            ) * 2 + [
+                [pltpu.VMEM((1, slots), jnp.int32)] * 4
+            ) + [
                 pltpu.VMEM((n_col, slots, wide), BF16),
                 pltpu.VMEM((slots, wide), BF16),
-                pltpu.VMEM((n_row, 2, slots, HALF), BF16),
+                pltpu.VMEM((chips, 2, slots, HALF), BF16),
                 pltpu.VMEM((n_col, 8, LANES), jnp.int32),
-                pltpu.VMEM((n_row, 8, LANES), jnp.int32),
+                pltpu.VMEM((chips, 8, LANES), jnp.int32),
                 pltpu.VMEM((8, LANES), jnp.int32),
                 pltpu.VMEM((8, LANES), jnp.int32),
                 pltpu.VMEM((n_row, RB * BS, 8 * BS), BF16),
@@ -383,24 +393,22 @@
                 pltpu.VMEM((8 * BS, 8 * BS), BF16),
                 pltpu.VMEM((4, 256, 256), F32),
                 pltpu.VMEM((4, LANES, LANES), F32),
-                pltpu.VMEM((4, 3, LANES, LANES), jnp.int16),
+                pltpu.VMEM((3, 4, LANES, LANES), jnp.int16),
                 pltpu.VMEM((4, 4, LANES, LANES), jnp.int16),
-                pltpu.VMEM((4, 3, 1, LANES), F32),
+                pltpu.VMEM((3, 4, 1, LANES), F32),
                 pltpu.VMEM((4, 4, 1, LANES), F32),
                 dma((8,)),
                 dma((n_col, 2)), dma((n_col, 2)), dma((n_col,)), dma((n_col,)),
                 dma((chips, 2)), dma((chips, 2)), dma((chips, 2)), dma((chips, 2)),
-                dma, dma,
-                dma((n_row,)), dma((n_row,)),
-                dma((4, 3)), dma((4, 4)), dma((4, 3)), dma((4, 4)),
+                dma((chips,)), dma((chips,)),
+                dma((3, 3)), dma((3, 4)), dma((3, 3)), dma((3, 4)),
             ],
             compiler_params=pltpu.CompilerParams(
-                collective_id=0, has_side_effects=True, vmem_limit_bytes=56_200_000
+                collective_id=0, has_side_effects=True, vmem_limit_bytes=40 * 2**20
             ),
         )(
-            a_vals.reshape(slots, wide), p_vals.reshape(slots, wide),
-            a_rows.reshape(1, slots), a_cols.reshape(1, slots), a_count.reshape(1, 1),
-            p_rows.reshape(1, slots), p_cols.reshape(1, slots), p_count.reshape(1, 1),
+            keep(a_vals, (slots, wide)), keep(p_vals, (slots, wide)), keep(a_rows, (1, slots)), keep(a_cols, (1, slots)),
+            keep(p_rows, (1, slots)), keep(p_cols, (1, slots)), a_count.reshape(1, 1), p_count.reshape(1, 1),
         )
         return got.transpose(1, 0, 2).reshape(RB * BS, LANES)
 

time: 30.2 us -> 28.3 us (0.937)
  Pallas kernels: 27.3 us -> 26.1 us
  local copies, waits for them, and re-layouts: 1.42 us -> 0.75 us
    pallas_call x1, Pallas kernels: 27.3 us -> 26.1 us  [on_device(): pl.pallas_call(functools.partial(kernel, n_row, n_col, n_layer), out_shap...]
    unnamed x8 -> x0, local copies, waits for them, and re-layouts: 0.67 us -> none
where the time goes in v3:
time: 28.3 us; the launch traced here: 28.2 us
  Pallas kernels  26.1 us (92%)
  between operations  1.3 us (5%)
  local copies, waits for them, and re-layouts  0.75 us (3%)
    pallas_call x1, Pallas kernels, on_device(): pl.pallas_call(functools.partial(kernel, n_row, n_col, n_layer), out_shap...  26.1 us
    transpose x1, local copies, waits for them, and re-layouts, on_device(): return got.transpose(1, 0, 2).reshape(RB * BS, LANES)  0.75 us

profile of v3, /device:TPU:0, one launch (start us, length us, event | category | flops | bytes accessed | tf_op | source)
XLA Modules:
  0.0 28.2 jit_solution(16919234802381994560)
XLA Ops:
  1.3 26.1 %shard_map.82 = f32[64,8,128]{2,1,0:T(8,128)S(1)} custom-call(bf16[32,4096]{1,0:T(8,128)(2,1)} %bitcast.13, bf16[32,4096]{1,0:T(8,128)(2,1)} %bitcast.14, s32[1,32]{1,0:T(1,128)} %bitcast.15, s32[1,32]{1,0:T(1,128)} %bitcast.16, s32[1,32]{1,0:T(1,128)} %bitcast.17, s32[1,32]{1,0:T(1,128)} %bitcast.18, s32[1,1]{1,0:T(1,128)} %bitcast.10.rest_4_, ...), custom_call_target="tpu_custom_call" | custom-call | tf_op jit(solution)/shard_map/pallas_call | solution.py:375
  27.4 0.8 %copy.9 = f32[8,64,128]{2,1,0:T(8,128)} copy(f32[8,64,128]{2,0,1:T(8,128)S(1)} %bitcast.12) | data formatting | bytes 524288 | tf_op jit(solution)/shard_map/transpose | solution.py:413

commit v4 on v3

--- a/solution.py
+++ b/solution.py
@@ -262,23 +262,32 @@
         for copy in copies:
             copy.wait_recv()
 
-    def ready(g):
+    both = (0, 1, 2)
+
+    def give(g, j, slot, to):
+        for k in groups[g]:
+            encode(k, j, packed(k, to))
+        return hand(g, j, slot, near if slot == 4 else to)
+
+    def give_far(g):
+        start(give(g, 2, 4 if g in both else 2, far))
+
+    def give_via(g):
         for k in groups[g]:
             encode(k, 0, packed(k, opposite))
         start(via(g))
 
-        @pl.when(jnp.logical_not(inner))
-        def _():
-            for k in groups[g]:
-                encode(k, 2, packed(k, far))
-            start(hand(g, 2, 2, far))
-
+    def ready(g):
+        if g in both:
+            pl.when(jnp.logical_not(inner))(functools.partial(give_via, g))
+        else:
+            give_via(g)
+        pl.when(jnp.logical_not(inner))(functools.partial(give_far, g))
         for k in groups[g]:
-            encode(k, 1, packed(k, near))
             total[k] = packed(k, lay)
 
     def send_near(g):
-        start(hand(g, 1, 1, near))
+        start(give(g, 1, 1, near))
 
     def forward(g):
         @pl.when(inner)
@@ -287,20 +296,24 @@
             for k in groups[g]:
                 encode(k, 2, packed(k, far) + decode(k, 0))
             start(hand(g, 2, 2, far))
+            if g in both:
+                arrive(hand(g, 0, 4, near))
+                for k in groups[g]:
+                    encode(k, 0, packed(k, opposite) + decode(k, 4))
+                start(hand(g, 0, 3, opposite))
+
+    def add(g, slot, to):
+        arrive(hand(g, 0, slot, to))
+        for k in groups[g]:
+            total[k] += decode(k, slot)
 
     def collect(g):
-        @pl.when(inner)
-        def _():
-            arrive(hand(g, 0, 3, opposite))
-            for k in groups[g]:
-                total[k] += decode(k, 3)
-
-        arrive(hand(g, 1, 1, near))
-        for k in groups[g]:
-            total[k] += decode(k, 1)
-        arrive(hand(g, 2, 2, far))
-        for k in groups[g]:
-            total[k] += decode(k, 2)
+        pl.when(inner)(functools.partial(add, g, 3, opposite))
+        add(g, 1, near)
+        if g in both:
+            pl.when(jnp.logical_not(inner))(functools.partial(add, g, 2, far))
+        else:
+            add(g, 2, far)
 
     def fill(h):
         for d in range(1, chips):
@@ -334,8 +347,8 @@
     multiply(2, 1, pl.ds(0, 512))
     ready(2)
     send_near(1)
+    send_near(2)
     forward(1)
-    send_near(2)
     forward(2)
     for g in range(3):
         collect(g)
@@ -394,14 +407,14 @@
                 pltpu.VMEM((4, 256, 256), F32),
                 pltpu.VMEM((4, LANES, LANES), F32),
                 pltpu.VMEM((3, 4, LANES, LANES), jnp.int16),
-                pltpu.VMEM((4, 4, LANES, LANES), jnp.int16),
+                pltpu.VMEM((5, 4, LANES, LANES), jnp.int16),
                 pltpu.VMEM((3, 4, 1, LANES), F32),
-                pltpu.VMEM((4, 4, 1, LANES), F32),
+                pltpu.VMEM((5, 4, 1, LANES), F32),
                 dma((8,)),
                 dma((n_col, 2)), dma((n_col, 2)), dma((n_col,)), dma((n_col,)),
                 dma((chips, 2)), dma((chips, 2)), dma((chips, 2)), dma((chips, 2)),
                 dma((chips,)), dma((chips,)),
-                dma((3, 3)), dma((3, 4)), dma((3, 3)), dma((3, 4)),
+                dma((3, 3)), dma((3, 5)), dma((3, 3)), dma((3, 5)),
             ],
             compiler_params=pltpu.CompilerParams(
                 collective_id=0, has_side_effects=True, vmem_limit_bytes=40 * 2**20

time: 28.3 us -> 28 us (0.989)
  Pallas kernels: 26.1 us -> 25.8 us
where the time goes in v4:
time: 28 us; the launch traced here: 27.9 us
  Pallas kernels  25.8 us (92%)
  between operations  1.3 us (5%)
  local copies, waits for them, and re-layouts  0.75 us (3%)
    pallas_call x1, Pallas kernels, on_device(): pl.pallas_call(functools.partial(kernel, n_row, n_col, n_layer), out_shap...  25.8 us
    transpose x1, local copies, waits for them, and re-layouts, on_device(): return got.transpose(1, 0, 2).reshape(RB * BS, LANES)  0.75 us

profile of v4, /device:TPU:0, one launch (start us, length us, event | category | flops | bytes accessed | tf_op | source)
XLA Modules:
  0.0 27.9 jit_solution(15741359962566149311)
XLA Ops:
  1.3 25.8 %shard_map.82 = f32[64,8,128]{2,1,0:T(8,128)S(1)} custom-call(bf16[32,4096]{1,0:T(8,128)(2,1)} %bitcast.13, bf16[32,4096]{1,0:T(8,128)(2,1)} %bitcast.14, s32[1,32]{1,0:T(1,128)} %bitcast.15, s32[1,32]{1,0:T(1,128)} %bitcast.16, s32[1,32]{1,0:T(1,128)} %bitcast.17, s32[1,32]{1,0:T(1,128)} %bitcast.18, s32[1,1]{1,0:T(1,128)} %bitcast.10.rest_4_, ...), custom_call_target="tpu_custom_call" | custom-call | tf_op jit(solution)/shard_map/pallas_call | solution.py:388
  27.1 0.8 %copy.9 = f32[8,64,128]{2,1,0:T(8,128)} copy(f32[8,64,128]{2,0,1:T(8,128)S(1)} %bitcast.12) | data formatting | bytes 524288 | tf_op jit(solution)/shard_map/transpose | solution.py:426

commit v5 on v4

--- a/solution.py
+++ b/solution.py
@@ -341,12 +341,13 @@
     fill(1)
     multiply(1, 0, pl.ds(256, 256))
     ready(1)
+    pl.when(inner)(lambda: send_near(1))
     forward(0)
     for d in range(chips):
         shared[d, 1].wait_recv()
     multiply(2, 1, pl.ds(0, 512))
     ready(2)
-    send_near(1)
+    pl.when(jnp.logical_not(inner))(lambda: send_near(1))
     send_near(2)
     forward(1)
     forward(2)

time: 28 us -> 28 us (level)
  no operation moved by 1% of the time
where the time goes in v5:
time: 28 us; the launch traced here: 27.8 us
  Pallas kernels  25.8 us (92%)
  between operations  1.3 us (5%)
  local copies, waits for them, and re-layouts  0.75 us (3%)
    pallas_call x1, Pallas kernels, on_device(): pl.pallas_call(functools.partial(kernel, n_row, n_col, n_layer), out_shap...  25.8 us
    transpose x1, local copies, waits for them, and re-layouts, on_device(): return got.transpose(1, 0, 2).reshape(RB * BS, LANES)  0.75 us

profile of v5, /device:TPU:0, one launch (start us, length us, event | category | flops | bytes accessed | tf_op | source)
XLA Modules:
  0.0 27.8 jit_solution(11345687604497108739)
XLA Ops:
  1.3 25.8 %shard_map.82 = f32[64,8,128]{2,1,0:T(8,128)S(1)} custom-call(bf16[32,4096]{1,0:T(8,128)(2,1)} %bitcast.13, bf16[32,4096]{1,0:T(8,128)(2,1)} %bitcast.14, s32[1,32]{1,0:T(1,128)} %bitcast.15, s32[1,32]{1,0:T(1,128)} %bitcast.16, s32[1,32]{1,0:T(1,128)} %bitcast.17, s32[1,32]{1,0:T(1,128)} %bitcast.18, s32[1,1]{1,0:T(1,128)} %bitcast.10.rest_4_, ...), custom_call_target="tpu_custom_call" | custom-call | tf_op jit(solution)/shard_map/pallas_call | solution.py:389
  27.1 0.8 %copy.9 = f32[8,64,128]{2,1,0:T(8,128)} copy(f32[8,64,128]{2,0,1:T(8,128)S(1)} %bitcast.12) | data formatting | bytes 524288 | tf_op jit(solution)/shard_map/transpose | solution.py:427

commit v6 on v5

--- a/solution.py
+++ b/solution.py
@@ -342,9 +342,9 @@
     multiply(1, 0, pl.ds(256, 256))
     ready(1)
     pl.when(inner)(lambda: send_near(1))
-    forward(0)
     for d in range(chips):
         shared[d, 1].wait_recv()
+    forward(0)
     multiply(2, 1, pl.ds(0, 512))
     ready(2)
     pl.when(jnp.logical_not(inner))(lambda: send_near(1))

time: 28 us -> 28 us (level)
  no operation moved by 1% of the time
where the time goes in v6:
time: 28 us; the launch traced here: 27.8 us
  Pallas kernels  25.8 us (92%)
  between operations  1.3 us (5%)
  local copies, waits for them, and re-layouts  0.75 us (3%)
    pallas_call x1, Pallas kernels, on_device(): pl.pallas_call(functools.partial(kernel, n_row, n_col, n_layer), out_shap...  25.8 us
    transpose x1, local copies, waits for them, and re-layouts, on_device(): return got.transpose(1, 0, 2).reshape(RB * BS, LANES)  0.75 us

profile of v6, /device:TPU:0, one launch (start us, length us, event | category | flops | bytes accessed | tf_op | source)
XLA Modules:
  0.0 27.8 jit_solution(2017754460973149204)
XLA Ops:
  1.3 25.8 %shard_map.82 = f32[64,8,128]{2,1,0:T(8,128)S(1)} custom-call(bf16[32,4096]{1,0:T(8,128)(2,1)} %bitcast.13, bf16[32,4096]{1,0:T(8,128)(2,1)} %bitcast.14, s32[1,32]{1,0:T(1,128)} %bitcast.15, s32[1,32]{1,0:T(1,128)} %bitcast.16, s32[1,32]{1,0:T(1,128)} %bitcast.17, s32[1,32]{1,0:T(1,128)} %bitcast.18, s32[1,1]{1,0:T(1,128)} %bitcast.10.rest_4_, ...), custom_call_target="tpu_custom_call" | custom-call | tf_op jit(solution)/shard_map/pallas_call | solution.py:389
  27.1 0.8 %copy.9 = f32[8,64,128]{2,1,0:T(8,128)} copy(f32[8,64,128]{2,0,1:T(8,128)S(1)} %bitcast.12) | data formatting | bytes 524288 | tf_op jit(solution)/shard_map/transpose | solution.py:427

commit v7 on v6

--- a/solution.py
+++ b/solution.py
@@ -344,9 +344,9 @@
     pl.when(inner)(lambda: send_near(1))
     for d in range(chips):
         shared[d, 1].wait_recv()
-    forward(0)
     multiply(2, 1, pl.ds(0, 512))
     ready(2)
+    forward(0)
     pl.when(jnp.logical_not(inner))(lambda: send_near(1))
     send_near(2)
     forward(1)

time: 28 us -> 28 us (level)
  no operation moved by 1% of the time
where the time goes in v7:
time: 28 us; the launch traced here: 27.8 us
  Pallas kernels  25.8 us (92%)
  between operations  1.3 us (5%)
  local copies, waits for them, and re-layouts  0.75 us (3%)
    pallas_call x1, Pallas kernels, on_device(): pl.pallas_call(functools.partial(kernel, n_row, n_col, n_layer), out_shap...  25.8 us
    transpose x1, local copies, waits for them, and re-layouts, on_device(): return got.transpose(1, 0, 2).reshape(RB * BS, LANES)  0.75 us

profile of v7, /device:TPU:0, one launch (start us, length us, event | category | flops | bytes accessed | tf_op | source)
XLA Modules:
  0.0 27.8 jit_solution(13828379998714364831)
XLA Ops:
  1.3 25.8 %shard_map.82 = f32[64,8,128]{2,1,0:T(8,128)S(1)} custom-call(bf16[32,4096]{1,0:T(8,128)(2,1)} %bitcast.13, bf16[32,4096]{1,0:T(8,128)(2,1)} %bitcast.14, s32[1,32]{1,0:T(1,128)} %bitcast.15, s32[1,32]{1,0:T(1,128)} %bitcast.16, s32[1,32]{1,0:T(1,128)} %bitcast.17, s32[1,32]{1,0:T(1,128)} %bitcast.18, s32[1,1]{1,0:T(1,128)} %bitcast.10.rest_4_, ...), custom_call_target="tpu_custom_call" | custom-call | tf_op jit(solution)/shard_map/pallas_call | solution.py:389
  27.1 0.8 %copy.9 = f32[8,64,128]{2,1,0:T(8,128)} copy(f32[8,64,128]{2,0,1:T(8,128)S(1)} %bitcast.12) | data formatting | bytes 524288 | tf_op jit(solution)/shard_map/transpose | solution.py:427
